TPU v7x, 32 devices: a whole 2x2x4 slice. The times are simulated.
32 devices in a mesh: blk: 8 (over z, x), rep: 4 (over y, core).
Axes of the slice: x: 2, y: 2, z: 4, core: 2. Of those that a mesh axis runs over, the one named last changes fastest.
Arguments:
- orbitals: bfloat16 [32, 32, 48, 128], P('blk'), may hold values from -6 to 6
- skew: int32 [4], P('rep'), may hold values from 0 to 7
Outputs:
- exchange_fields: float32 [32, 32, 48, 128], P('blk', 'rep')
All inputs are finite; a program needn't handle non-finite values.
Results may differ from a plain program's by a relative error of at most 0.0041.
Values may be sent and summed in bfloat16 or wider, within the bound.
A program may use at most 64 MiB of HBM per device.

v0:
```python
import math

import jax
import jax.numpy as jnp
from jax import lax
from jax.sharding import PartitionSpec as P

NX = 32
NY = 48
NZ = 128
HOPS = 4


def shifted_2(value, axis, steps):
    count = lax.axis_size(axis)
    pairs = [(source, (source + steps) % count) for source in range(count)]
    return lax.ppermute(value, axis, pairs)


def cas_table(length):
    indices = jnp.arange(length, dtype=jnp.int32)
    products = indices[:, None] * indices[None, :] % length
    angles = 2.0 * math.pi / length * products.astype(jnp.float32)
    return (jnp.cos(angles) + jnp.sin(angles)).astype(jnp.bfloat16)


def frequency_squares(length):
    indices = jnp.arange(length, dtype=jnp.int32)
    signed = jnp.where(indices > length // 2, indices - length, indices)
    wave = 2.0 * math.pi / length * signed.astype(jnp.float32)
    return wave * wave


def kernel_table():
    squares = (
        frequency_squares(NX)[:, None, None]
        + frequency_squares(NY)[None, :, None]
        + frequency_squares(NZ)[None, None, :]
    )
    safe_sq = jnp.where(squares > 0, squares, 1.0)
    kernel = jnp.where(
        squares > 0, 4.0 * math.pi * (1.0 - jnp.exp(-squares)) / safe_sq, 4.0 * math.pi
    )
    return kernel / (NX * NY * NZ)


def transform(field, table_x, table_y, table_z):
    first = jnp.einsum("oxyz,zk->oxyk", field, table_z, preferred_element_type=jnp.float32).astype(
        jnp.bfloat16
    )
    second = jnp.einsum("oxyz,yk->oxkz", first, table_y, preferred_element_type=jnp.float32).astype(
        jnp.bfloat16
    )
    return jnp.einsum("oxyz,xk->okyz", second, table_x, preferred_element_type=jnp.float32)


def pair_field(residents, visitor, table_x, table_y, table_z, kernel):
    density = (residents.astype(jnp.float32) * visitor.astype(jnp.float32)[None]).astype(
        jnp.bfloat16
    )
    forward = transform(density, table_x, table_y, table_z).astype(jnp.bfloat16)
    scaled = (kernel[None] * forward.astype(jnp.float32)).astype(jnp.bfloat16)
    potential = transform(scaled, table_x, table_y, table_z)
    return potential * visitor.astype(jnp.float32)[None]


def shift_by(visitor, offset):
    for level in range((lax.axis_size("blk") - 1).bit_length()):
        shifted = shifted_2(visitor, "blk", 1 << level)
        visitor = jnp.where(offset // (1 << level) % 2 == 1, shifted, visitor)
    return visitor


def body(orbitals, skew):
    table_x = cas_table(NX)
    table_y = cas_table(NY)
    table_z = cas_table(NZ)
    kernel = kernel_table()
    replica = lax.axis_index("rep")
    start_orb = lax.dynamic_index_in_dim(orbitals, replica % orbitals.shape[0], 0, keepdims=False)
    field_sum = jnp.zeros(orbitals.shape, jnp.float32)
    visitor = shift_by(start_orb, skew[0])
    for hop_index in range(HOPS):
        if hop_index > 0:
            visitor = shifted_2(visitor, "blk", 1)
        field_sum = field_sum + pair_field(orbitals, visitor, table_x, table_y, table_z, kernel)
    return lax.psum_scatter(field_sum, "rep", scatter_dimension=1, tiled=True)


def solution(mesh):
    placed = (P("blk", None, None, None), P("rep"))
    return jax.shard_map(
        body, mesh=mesh, in_specs=placed, out_specs=P("blk", "rep", None, None), check_vma=False
    )
```

profile of v0, /device:TPU:0, one launch (start us, length us, event | category | flops | bytes accessed | tf_op | source)
XLA Modules:
  0.0 188.9 jit_solution(17126558872366489148)
XLA Ops:
  6.5 0.0 reduce-scatter.2.cloned.1.call-start
  6.5 1.0 dynamic-slice_bitcast_fusion
  7.6 3.0 %collective-permute-start = (bf16[32,48,128]{2,1,0:T(8,128)(2,1)S(1)}, bf16[32,48,128]{2,1,0:T(8,128)(2,1)S(1)}, u32[]{:S(2)}, u32[]{:S(2)}) collective-permute-start(bf16[32,48,128]{2,1,0:T(8,128)(2,1)S(1)} %dynamic-slice_bitcast_fusion), channel_id=1, source_target_pairs={{0,4},{4,8},{8,12},{12,16},{16,20},{20,24},{24,28},{28,0},{1,5},{5... | collective-permute-start | bytes 1179656 | tf_op jit(solution)/shard_map/ppermute | solution.py:17
  11.2 11.5 %collective-permute-done = bf16[32,48,128]{2,1,0:T(8,128)(2,1)S(1)} collective-permute-done((bf16[32,48,128]{2,1,0:T(8,128)(2,1)S(1)}, bf16[32,48,128]{2,1,0:T(8,128)(2,1)S(1)}, u32[]{:S(2)}, u32[]{:S(2)}) %collective-permute-start) | collective-permute-done | bytes 393248 | tf_op jit(solution)/shard_map/ppermute | solution.py:17
  22.7 1.0 broadcast_select_fusion
  23.7 0.1 collective-permute-start.1
  23.9 12.0 %collective-permute-done.1 = bf16[32,48,128]{2,1,0:T(8,128)(2,1)S(1)} collective-permute-done((bf16[32,48,128]{2,1,0:T(8,128)(2,1)S(1)}, bf16[32,48,128]{2,1,0:T(8,128)(2,1)S(1)}, u32[]{:S(2)}, u32[]{:S(2)}) %collective-permute-start.1) | collective-permute-done | bytes 393248 | tf_op jit(solution)/shard_map/ppermute | solution.py:17
  35.9 0.0 copy-start
  36.0 0.1 collective-permute-start.2
  36.0 0.1 broadcast_add_fusion
  36.1 1.3 fusion.69
  37.5 15.5 %collective-permute-done.2 = bf16[32,48,128]{2,1,0:T(8,128)(2,1)S(1)} collective-permute-done((bf16[32,48,128]{2,1,0:T(8,128)(2,1)S(1)}, bf16[32,48,128]{2,1,0:T(8,128)(2,1)S(1)}, u32[]{:S(2)}, u32[]{:S(2)}) %collective-permute-start.2) | collective-permute-done | bytes 393248 | tf_op jit(solution)/shard_map/ppermute | solution.py:17
  52.9 0.8 fusion.347
  53.8 0.0 collective-permute-start.3
  53.8 2.6 %fusion.57 = bf16[48,4,32,128]{3,0,2,1:T(8,128)(2,1)} fusion(bf16[4,32,48,128]{3,2,1,0:T(8,128)(2,1)S(1)} %copy-done, f32[32,48,128]{2,1,0:T(8,128)S(1)} %get-tuple-element.5), kind=kOutput, calls=%fused_computation.69 | convolution fusion | flops 280257280 | bytes 3932160 | tf_op jit(solution)/shard_map/oxyz,yk->oxkz/dot_general | solution.py:51
  56.4 2.0 %copy.8 = f32[32,48,128]{2,0,1:T(8,128)} copy(bf16[32,48,128]{2,1,0:T(8,128)(2,1)} %get-tuple-element.6) | data formatting | bytes 1179648 | tf_op jit(solution)/shard_map/convert_element_type | solution.py:58
  58.4 2.1 %fusion.38 = bf16[32,4,48,128]{3,0,2,1:T(8,128)(2,1)S(1)} fusion(bf16[48,4,32,128]{3,0,2,1:T(8,128)(2,1)} %fusion.57), kind=kOutput, calls=%fused_computation.59 | convolution fusion | flops 50348032 | bytes 3145728 | tf_op jit(solution)/shard_map/oxyz,xk->okyz/dot_general | solution.py:54
  60.4 7.3 %collective-permute-done.3 = bf16[32,48,128]{2,1,0:T(8,128)(2,1)S(1)} collective-permute-done((bf16[32,48,128]{2,1,0:T(8,128)(2,1)}, bf16[32,48,128]{2,1,0:T(8,128)(2,1)S(1)}, u32[]{:S(2)}, u32[]{:S(2)}) %collective-permute-start.3) | collective-permute-done | bytes 393248 | tf_op jit(solution)/shard_map/ppermute | solution.py:17
  67.7 0.0 collective-permute-start.4
  67.7 0.9 convert_element_type.325
  68.7 3.7 %fusion.60 = bf16[48,4,32,128]{3,0,2,1:T(8,128)(2,1)} fusion(bf16[4,32,48,128]{3,2,1,0:T(8,128)(2,1)S(1)} %copy-done, f32[32,48,128]{2,1,0:T(8,128)} %convert_element_type.325), kind=kOutput, calls=%fused_computation.70 | convolution fusion | flops 280257280 | bytes 3932160 | tf_op jit(solution)/shard_map/oxyz,yk->oxkz/dot_general | solution.py:51
  72.4 1.0 copy.9
  73.4 3.2 %fusion.35 = bf16[32,4,48,128]{3,0,2,1:T(8,128)(2,1)} fusion(bf16[48,4,32,128]{3,0,2,1:T(8,128)(2,1)} %fusion.60), kind=kOutput, calls=%fused_computation.56 | convolution fusion | flops 50348032 | bytes 3145728 | tf_op jit(solution)/shard_map/oxyz,xk->okyz/dot_general | solution.py:54
  76.6 4.1 %collective-permute-done.4 = bf16[32,48,128]{2,1,0:T(8,128)(2,1)} collective-permute-done((bf16[32,48,128]{2,1,0:T(8,128)(2,1)S(1)}, bf16[32,48,128]{2,1,0:T(8,128)(2,1)}, u32[]{:S(2)}, u32[]{:S(2)}) %collective-permute-start.4) | collective-permute-done | bytes 393248 | tf_op jit(solution)/shard_map/ppermute | solution.py:17
  80.7 0.0 collective-permute-start.5
  80.7 2.0 %convert_element_type.337 = f32[32,48,128]{2,1,0:T(8,128)} convert(bf16[32,48,128]{2,1,0:T(8,128)(2,1)} %collective-permute-done.4) | non-fusion elementwise | flops 196608 | bytes 1179648 | tf_op jit(solution)/shard_map/convert_element_type | solution.py:58
  82.7 3.7 %fusion.63 = bf16[48,4,32,128]{3,0,2,1:T(8,128)(2,1)} fusion(bf16[4,32,48,128]{3,2,1,0:T(8,128)(2,1)S(1)} %copy-done, f32[32,48,128]{2,1,0:T(8,128)} %convert_element_type.337), kind=kOutput, calls=%fused_computation.71 | convolution fusion | flops 280257280 | bytes 3932160 | tf_op jit(solution)/shard_map/oxyz,yk->oxkz/dot_general | solution.py:51
  86.4 2.0 %copy.10 = f32[32,48,128]{2,0,1:T(8,128)} copy(bf16[32,48,128]{2,1,0:T(8,128)(2,1)} %collective-permute-done.4) | data formatting | bytes 1179648 | tf_op jit(solution)/shard_map/convert_element_type | solution.py:58
  88.3 3.2 %fusion.32 = bf16[32,4,48,128]{3,0,2,1:T(8,128)(2,1)} fusion(bf16[48,4,32,128]{3,0,2,1:T(8,128)(2,1)} %fusion.63), kind=kOutput, calls=%fused_computation.53 | convolution fusion | flops 50348032 | bytes 3145728 | tf_op jit(solution)/shard_map/oxyz,xk->okyz/dot_general | solution.py:54
  91.5 1.3 collective-permute-done.5
  92.9 0.9 convert_element_type.349
  93.8 3.7 %fusion.66 = bf16[48,4,32,128]{3,0,2,1:T(8,128)(2,1)} fusion(bf16[4,32,48,128]{3,2,1,0:T(8,128)(2,1)S(1)} %copy-done, f32[32,48,128]{2,1,0:T(8,128)} %convert_element_type.349), kind=kOutput, calls=%fused_computation.72 | convolution fusion | flops 280257280 | bytes 3932160 | tf_op jit(solution)/shard_map/oxyz,yk->oxkz/dot_general | solution.py:51
  97.5 2.2 %fusion.29 = bf16[32,4,48,128]{3,0,2,1:T(8,128)(2,1)S(1)} fusion(bf16[48,4,32,128]{3,0,2,1:T(8,128)(2,1)} %fusion.66), kind=kOutput, calls=%fused_computation.50 | convolution fusion | flops 50348032 | bytes 3145728 | tf_op jit(solution)/shard_map/oxyz,xk->okyz/dot_general | solution.py:54
  99.8 0.1 copy-done.2
  99.9 9.0 %fusion.7 = (bf16[4,32,48,128]{3,2,0,1:T(8,128)(2,1)}, bf16[4,32,48,128]{3,2,0,1:T(8,128)(2,1)}, bf16[4,32,48,128]{3,2,0,1:T(8,128)(2,1)}, bf16[4,32,48,128]{3,2,0,1:T(8,128)(2,1)S(1)}) fusion(bf16[32,4,48,128]{3,0,2,1:T(8,128)(2,1)S(1)} %fusion.29, f32[32,48,128]{2,1,0:T(8,128)} %fusion.69, bf16[32,4,48,128]{3,0,2,1:T(8,128)(2,1)S(1)} %copy-done.1, ...), kind=kLoop, calls=%fused_computation.36 | loop fusion | flops 9437184 | bytes 13369344 | tf_op jit(solution)/shard_map/convert_element_type | solution.py:62
  108.9 2.5 %fusion.45 = bf16[48,4,32,128]{3,0,2,1:T(8,128)(2,1)} fusion(bf16[4,32,48,128]{3,2,0,1:T(8,128)(2,1)S(1)} %get-tuple-element.10), kind=kOutput, calls=%fused_computation.65 | convolution fusion | flops 277897984 | bytes 3145728 | tf_op jit(solution)/shard_map/oxyz,yk->oxkz/dot_general | solution.py:51
  111.4 2.1 %fusion.10 = f32[32,4,48,128]{3,0,2,1:T(8,128)S(1)} fusion(bf16[48,4,32,128]{3,0,2,1:T(8,128)(2,1)} %fusion.45), kind=kOutput, calls=%fused_computation.39 | convolution fusion | flops 50348032 | bytes 4718592 | tf_op jit(solution)/shard_map/oxyz,xk->okyz/dot_general | solution.py:54
  113.5 4.0 %fusion.48 = bf16[48,4,32,128]{3,0,2,1:T(8,128)(2,1)} fusion(bf16[4,32,48,128]{3,2,0,1:T(8,128)(2,1)} %get-tuple-element.8), kind=kOutput, calls=%fused_computation.66 | convolution fusion | flops 277897984 | bytes 3145728 | tf_op jit(solution)/shard_map/oxyz,yk->oxkz/dot_general | solution.py:51
  117.5 3.7 %fusion.14 = f32[32,4,48,128]{3,0,2,1:T(8,128)} fusion(bf16[48,4,32,128]{3,0,2,1:T(8,128)(2,1)} %fusion.48), kind=kOutput, calls=%fused_computation.42 | convolution fusion | flops 50348032 | bytes 4718592 | tf_op jit(solution)/shard_map/oxyz,xk->okyz/dot_general | solution.py:54
  121.2 4.0 %fusion.51 = bf16[48,4,32,128]{3,0,2,1:T(8,128)(2,1)} fusion(bf16[4,32,48,128]{3,2,0,1:T(8,128)(2,1)} %get-tuple-element.9), kind=kOutput, calls=%fused_computation.67 | convolution fusion | flops 277897984 | bytes 3145728 | tf_op jit(solution)/shard_map/oxyz,yk->oxkz/dot_general | solution.py:51
  125.2 3.7 %fusion.18 = f32[32,4,48,128]{3,0,2,1:T(8,128)} fusion(bf16[48,4,32,128]{3,0,2,1:T(8,128)(2,1)} %fusion.51), kind=kOutput, calls=%fused_computation.45 | convolution fusion | flops 50348032 | bytes 4718592 | tf_op jit(solution)/shard_map/oxyz,xk->okyz/dot_general | solution.py:54
  128.9 4.0 %fusion.54 = bf16[48,4,32,128]{3,0,2,1:T(8,128)(2,1)} fusion(bf16[4,32,48,128]{3,2,0,1:T(8,128)(2,1)} %get-tuple-element.7), kind=kOutput, calls=%fused_computation.68 | convolution fusion | flops 277897984 | bytes 3145728 | tf_op jit(solution)/shard_map/oxyz,yk->oxkz/dot_general | solution.py:51
  132.9 0.1 copy.11
  133.1 1.0 copy-done.3
  134.1 8.0 %add_bitcast_fusion = f32[4,32,48,128]{3,1,2,0:T(8,128)} fusion(f32[32,4,48,128]{3,0,2,1:T(8,128)} %fusion.18, f32[32,4,48,128]{3,0,2,1:T(8,128)} %fusion.14, f32[32,4,48,128]{3,0,2,1:T(8,128)S(1)} %fusion.10, f32[32,48,128]{2,0,1:T(8,128)S(1)} %copy.11, f32[32,48,128]{2,0,1:T(8,128)} %copy.10, f32[32,48,128]{2,0,1:T(8,128)} %copy.9, ...), kind=kOutput, calls=%fused_computation.20 | convolution fusion | flops 55853056 | bytes 17301504 | tf_op jit(solution)/shard_map/oxyz,xk->okyz/dot_general | solution.py:54
  142.1 0.0 reduce-scatter.2.cloned.1.call-update
  142.1 37.8 %reduce-scatter.2.cloned.1.call-done = f32[4,8,48,128]{3,1,2,0:T(8,128)} async-done(((f32[4,32,48,128]{3,1,2,0:T(8,128)}), f32[4,8,48,128]{3,1,2,0:T(8,128)}) %reduce-scatter.2.cloned.1.call-update) | async-done | bytes 786448 | tf_op jit(solution)/shard_map/reduce_scatter | solution.py:87
  179.9 2.2 %copy.12 = f32[4,8,48,128]{3,2,1,0:T(8,128)} copy(f32[4,8,48,128]{3,1,2,0:T(8,128)} %reduce-scatter.2.cloned.1.call-done) | data formatting | bytes 1572864 | tf_op jit(solution)/shard_map/reduce_scatter | solution.py:87
  (9 shorter events, 0.1 us)
Async XLA Ops:
  6.5 173.4 %reduce-scatter.2.cloned.1.call-start = ((), (), s32[]{:S(2)}) async-start(), calls=%async_computation.1 | async-start | bytes 3932160 | tf_op jit(solution)/shard_map/reduce_scatter | solution.py:87
  7.6 15.1 %collective-permute-start = (bf16[32,48,128]{2,1,0:T(8,128)(2,1)S(1)}, bf16[32,48,128]{2,1,0:T(8,128)(2,1)S(1)}, u32[]{:S(2)}, u32[]{:S(2)}) collective-permute-start(bf16[32,48,128]{2,1,0:T(8,128)(2,1)S(1)} %dynamic-slice_bitcast_fusion), channel_id=1, source_target_pairs={{0,4},{4,8},{8,12},{12,16},{16,20},{20,24},{24,28},{28,0},{1,5},{5... | collective-permute-start | bytes 1179656 | tf_op jit(solution)/shard_map/ppermute | solution.py:17
  23.7 12.2 %collective-permute-start.1 = (bf16[32,48,128]{2,1,0:T(8,128)(2,1)S(1)}, bf16[32,48,128]{2,1,0:T(8,128)(2,1)S(1)}, u32[]{:S(2)}, u32[]{:S(2)}) collective-permute-start(bf16[32,48,128]{2,1,0:T(8,128)(2,1)S(1)} %broadcast_select_fusion), channel_id=1, source_target_pairs={{0,8},{4,12},{8,16},{12,20},{16,24},{20,28},{24,0},{28,4},{1,9},{5... | collective-permute-start | bytes 1179656 | tf_op jit(solution)/shard_map/ppermute | solution.py:17
  35.9 17.8 %copy-start = (bf16[4,32,48,128]{3,2,1,0:T(8,128)(2,1)S(1)}, bf16[4,32,48,128]{3,2,1,0:T(8,128)(2,1)}, u32[]{:S(2)}) copy-start(bf16[4,32,48,128]{3,2,1,0:T(8,128)(2,1)} %param.2) | copy-start | bytes 4718596
  36.0 17.0 %collective-permute-start.2 = (bf16[32,48,128]{2,1,0:T(8,128)(2,1)S(1)}, bf16[32,48,128]{2,1,0:T(8,128)(2,1)S(1)}, u32[]{:S(2)}, u32[]{:S(2)}) collective-permute-start(bf16[32,48,128]{2,1,0:T(8,128)(2,1)S(1)} %broadcast_select_fusion.1), channel_id=1, source_target_pairs={{0,16},{4,20},{8,24},{12,28},{16,0},{20,4},{24,8},{28,12},{1,17},{... | collective-permute-start | bytes 1179656 | tf_op jit(solution)/shard_map/ppermute | solution.py:17
  53.8 13.9 %collective-permute-start.3 = (bf16[32,48,128]{2,1,0:T(8,128)(2,1)}, bf16[32,48,128]{2,1,0:T(8,128)(2,1)S(1)}, u32[]{:S(2)}, u32[]{:S(2)}) collective-permute-start(bf16[32,48,128]{2,1,0:T(8,128)(2,1)} %get-tuple-element.6), channel_id=1, source_target_pairs={{0,4},{4,8},{8,12},{12,16},{16,20},{20,24},{24,28},{28,0},{1,5},{5... | collective-permute-start | bytes 1179656 | tf_op jit(solution)/shard_map/ppermute | solution.py:17
  67.7 13.0 %collective-permute-start.4 = (bf16[32,48,128]{2,1,0:T(8,128)(2,1)S(1)}, bf16[32,48,128]{2,1,0:T(8,128)(2,1)}, u32[]{:S(2)}, u32[]{:S(2)}) collective-permute-start(bf16[32,48,128]{2,1,0:T(8,128)(2,1)S(1)} %collective-permute-done.3), channel_id=1, source_target_pairs={{0,4},{4,8},{8,12},{12,16},{16,20},{20,24},{24,28},{28,0},{1,5},{5... | collective-permute-start | bytes 1179656 | tf_op jit(solution)/shard_map/ppermute | solution.py:17
  80.7 12.2 %collective-permute-start.5 = (bf16[32,48,128]{2,1,0:T(8,128)(2,1)}, bf16[32,48,128]{2,1,0:T(8,128)(2,1)S(1)}, u32[]{:S(2)}, u32[]{:S(2)}) collective-permute-start(bf16[32,48,128]{2,1,0:T(8,128)(2,1)} %collective-permute-done.4), channel_id=1, source_target_pairs={{0,4},{4,8},{8,12},{12,16},{16,20},{20,24},{24,28},{28,0},{1,5},{5... | collective-permute-start | bytes 1179656 | tf_op jit(solution)/shard_map/ppermute | solution.py:17
  97.5 2.2 %copy-start.1 = (bf16[32,4,48,128]{3,0,2,1:T(8,128)(2,1)S(1)}, bf16[32,4,48,128]{3,0,2,1:T(8,128)(2,1)}, u32[]{:S(2)}) copy-start(bf16[32,4,48,128]{3,0,2,1:T(8,128)(2,1)} %fusion.35) | copy-start | bytes 4718596
  97.5 2.4 %copy-start.2 = (bf16[32,4,48,128]{3,0,2,1:T(8,128)(2,1)S(1)}, bf16[32,4,48,128]{3,0,2,1:T(8,128)(2,1)}, u32[]{:S(2)}) copy-start(bf16[32,4,48,128]{3,0,2,1:T(8,128)(2,1)} %fusion.32) | copy-start | bytes 4718596
  132.9 1.1 copy-start.3
Sparse Core Ops, SparseCore 0:
  142.2 37.6 reduce-scatter.1
where the time goes:
time: 190 us; the launch traced here: 189 us
  waiting for transfers between devices  89.6 us (47%)
  matrix products  56.5 us (30%)
  other arithmetic  16.1 us (8%)
  between operations  14.2 us (7%)
  local copies, waits for them, and re-layouts  9.37 us (5%)
  starting transfers between devices  3.13 us (2%)
    ppermute x6, waiting for transfers between devices, shifted_2(): return lax.ppermute(value, axis, pairs)  51.7 us
    reduce_scatter x1, waiting for transfers between devices, body(): return lax.psum_scatter(field_sum, 'rep', scatter_dimension=1, tiled=True)  37.8 us
    dot_general x8, matrix products, transform(): jnp.einsum('oxyz,yk->oxkz', first, table_y, preferred_element_type=jnp.fl...  28.3 us
    dot_general x8, matrix products, transform(): jnp.einsum('oxyz,xk->okyz', second, table_x, preferred_element_type=jnp.f...  28.2 us
    convert_element_type x1, other arithmetic, pair_field(): scaled = (kernel[None] * forward.astype(jnp.float32)).astype(jnp.bfloat16)  8.97 us
    convert_element_type x4, local copies, waits for them, and re-layouts, pair_field(): visitor.astype(jnp.float32)[None]  5.03 us
    convert_element_type x4, other arithmetic, pair_field(): visitor.astype(jnp.float32)[None]  4.65 us
  transfers between devices with their start and end apart: 7, of which 7 were waited for; matrix products, arithmetic and copies ran while one was open for 15% of the time, Pallas kernels for 0%

commit v1 on v0

v1 whole, which is shorter than its diff:
```python
import functools
import math

import jax
import jax.numpy as jnp
import ml_dtypes
import numpy as np
from jax import lax
from jax.experimental import pallas as pl
from jax.experimental.pallas import tpu as pltpu
from jax.sharding import PartitionSpec as P

HOPS = 4
GROUP = 8
ROWS = 4
COLS = 2
CORES = 2
MESH = pl.DeviceIdType.MESH


def cas_table(length):
    indices = np.arange(length, dtype=np.int32)
    products = indices[:, None] * indices[None, :] % length
    angles = np.float32(2.0 * math.pi / length) * products.astype(np.float32)
    return (np.cos(angles) + np.sin(angles)).astype(ml_dtypes.bfloat16)


def frequency_squares(length):
    indices = np.arange(length, dtype=np.int32)
    signed = np.where(indices > length // 2, indices - length, indices)
    wave = np.float32(2.0 * math.pi / length) * signed.astype(np.float32)
    return wave * wave


def kernel_table(nx, ny, nz):
    squares = (
        frequency_squares(nx)[:, None, None]
        + frequency_squares(ny)[None, :, None]
        + frequency_squares(nz)[None, None, :]
    )
    safe_sq = np.where(squares > 0, squares, np.float32(1.0))
    kernel = np.where(
        squares > 0,
        np.float32(4.0 * math.pi) * -np.expm1(-squares) / safe_sq,
        np.float32(4.0 * math.pi),
    )
    return (kernel / np.float32(nx * ny * nz)).astype(np.float32)


def shifted_2(value, axis, steps):
    count = lax.axis_size(axis)
    pairs = [(source, (source + steps) % count) for source in range(count)]
    return lax.ppermute(value, axis, pairs)


def transform(field, table_x, table_y, table_z):
    first = jnp.einsum("oxyz,zk->oxyk", field, table_z, preferred_element_type=jnp.float32).astype(
        jnp.bfloat16
    )
    second = jnp.einsum("oxyz,yk->oxkz", first, table_y, preferred_element_type=jnp.float32).astype(
        jnp.bfloat16
    )
    return jnp.einsum("oxyz,xk->okyz", second, table_x, preferred_element_type=jnp.float32)


def pair_field(residents, visitor, tables, kernel):
    density = (residents.astype(jnp.float32) * visitor.astype(jnp.float32)[None]).astype(
        jnp.bfloat16
    )
    forward = transform(density, *tables).astype(jnp.bfloat16)
    scaled = (kernel[None] * forward.astype(jnp.float32)).astype(jnp.bfloat16)
    potential = transform(scaled, *tables)
    return potential * visitor.astype(jnp.float32)[None]


def shift_by(visitor, offset):
    for level in range((lax.axis_size("blk") - 1).bit_length()):
        shifted = shifted_2(visitor, "blk", 1 << level)
        visitor = jnp.where(offset // (1 << level) % 2 == 1, shifted, visitor)
    return visitor


def shift_body(orbitals, skew):
    _, nx, ny, nz = orbitals.shape
    tables = [jnp.asarray(cas_table(n)) for n in (nx, ny, nz)]
    kernel = jnp.asarray(kernel_table(nx, ny, nz))
    replica = lax.axis_index("rep")
    start_orb = lax.dynamic_index_in_dim(orbitals, replica % orbitals.shape[0], 0, keepdims=False)
    field_sum = jnp.zeros(orbitals.shape, jnp.float32)
    visitor = shift_by(start_orb, skew[0])
    for hop_index in range(HOPS):
        if hop_index > 0:
            visitor = shifted_2(visitor, "blk", 1)
        field_sum = field_sum + pair_field(orbitals, visitor, tables, kernel)
    return lax.psum_scatter(field_sum, "rep", scatter_dimension=1, tiled=True)


def fields_kernel(
    n_blk, n_rep, skew_ref, orb, tz_ref, ty_ref, tyt_ref, tx_ref, kern_ref, out_ref, *scratch
):
    n_orb, nx, ny, nz = orb.shape
    chunks = nx // ROWS
    levels = n_blk // COLS
    chips = n_rep // CORES
    per_slab = nx // n_rep // ROWS
    groups = ny // GROUP
    rows = ROWS * ny
    sub = ROWS * GROUP
    others = HOPS // COLS
    halves = n_orb // 2
    columns = scratch[:chunks]
    staged = scratch[chunks : 2 * chunks]
    sides = scratch[2 * chunks : 3 * chunks]
    scratch = scratch[3 * chunks :]
    vis, freq, send_core, recv_core, send_chip, recv_chip = scratch[:6]
    line_send, line_recv, side_send, side_recv, core_send, core_recv, chip_send, chip_recv = scratch[
        6:
    ]

    blk = lax.axis_index("blk")
    rep = lax.axis_index("rep")
    level, col = blk // COLS, blk % COLS
    chip, core = rep // CORES, rep % CORES
    side_blk = level * COLS + (COLS - 1 - col)
    core_rep = chip * CORES + (CORES - 1 - core)
    mine = rep % n_orb
    skew = skew_ref[0]

    def chip_rep(step):
        return (chip + step) % chips * CORES + core

    barrier = pltpu.get_barrier_semaphore()
    pl.semaphore_signal(barrier, inc=1, device_id=(side_blk, rep), device_id_type=MESH)
    pl.semaphore_signal(barrier, inc=1, device_id=(blk, core_rep), device_id_type=MESH)
    for step in range(1, chips):
        pl.semaphore_signal(barrier, inc=1, device_id=(blk, chip_rep(step)), device_id_type=MESH)

    @pl.when(level > 0)
    def _():
        pl.semaphore_signal(barrier, inc=1, device_id=(blk - COLS, rep), device_id_type=MESH)

    @pl.when(level < levels - 1)
    def _():
        pl.semaphore_signal(barrier, inc=1, device_id=(blk + COLS, rep), device_id_type=MESH)

    ends = (level == 0).astype(jnp.int32) + (level == levels - 1).astype(jnp.int32)
    pl.semaphore_wait(barrier, 2 + (chips - 1) + 2 - ends)

    def line_copy(c, hop, up):
        source = level - (hop - 1) if up else level + (hop - 1)
        way = 0 if up else 1
        if hop == 1:
            src = orb.at[mine, pl.ds(c * ROWS, ROWS)]
        else:
            src = columns[c].at[source]
        return pltpu.make_async_remote_copy(
            src_ref=src,
            dst_ref=columns[c].at[source],
            send_sem=line_send.at[c, hop - 1, way],
            recv_sem=line_recv.at[c, hop - 1, way],
            device_id=(blk + COLS if up else blk - COLS, rep),
            device_id_type=MESH,
        )

    def line_sends(c, hop, act):
        @pl.when((level < levels - 1) & (level >= hop - 1))
        def _():
            act(line_copy(c, hop, True))

        @pl.when((level > 0) & (level + hop - 1 <= levels - 1))
        def _():
            act(line_copy(c, hop, False))

    def line_arrivals(c, hop):
        def arrival(source, way):
            return pltpu.make_async_remote_copy(
                src_ref=columns[c].at[source],
                dst_ref=columns[c].at[source],
                send_sem=line_send.at[c, hop - 1, way],
                recv_sem=line_recv.at[c, hop - 1, way],
                device_id=(side_blk, rep),
                device_id_type=MESH,
            )

        @pl.when(level >= hop)
        def _():
            arrival(level - hop, 0).wait_recv()

        @pl.when(level + hop <= levels - 1)
        def _():
            arrival(level + hop, 1).wait_recv()

    def side_copy(c):
        return pltpu.make_async_remote_copy(
            src_ref=staged[c],
            dst_ref=sides[c],
            send_sem=side_send.at[c],
            recv_sem=side_recv.at[c],
            device_id=(side_blk, rep),
            device_id_type=MESH,
        )

    def send_side(c):
        first = (side_blk - skew - col) % COLS
        for j in range(others):
            owner = (side_blk - skew - first - COLS * j) % n_blk
            staged[c][j] = columns[c][owner // COLS]
        side_copy(c).start()

    def forward(c):
        for hop in range(HOPS):
            owner = (blk - skew - hop) % n_blk
            vis[hop, pl.ds(c * ROWS, ROWS)] = jnp.where(
                owner % COLS == col, columns[c][owner // COLS], sides[c][hop // COLS]
            )

        def unit(hop, carry):
            visitor = vis[hop, pl.ds(c * ROWS, ROWS)].reshape(rows, nz)
            for half in range(halves):
                density = jnp.concatenate(
                    [
                        orb[2 * half + k, pl.ds(c * ROWS, ROWS)].reshape(rows, nz) * visitor
                        for k in range(2)
                    ],
                    axis=1,
                )
                first = jnp.dot(density, tz_ref[...], preferred_element_type=jnp.float32)
                second = jnp.dot(
                    ty_ref[...], first.astype(jnp.bfloat16), preferred_element_type=jnp.float32
                )
                freq[hop * halves + half, :, pl.ds(c * sub, sub)] = second.astype(
                    jnp.bfloat16
                ).reshape(groups, sub, 2 * nz)
            return carry

        lax.fori_loop(0, HOPS, unit, 0)

    def middle():
        def unit(step, carry):
            group, hop = step // HOPS, step % HOPS
            factor = kern_ref[group]
            for half in range(halves):
                index = hop * halves + half
                third = jnp.dot(
                    tx_ref[...], freq[index, group], preferred_element_type=jnp.float32
                )
                scaled = jnp.concatenate(
                    [third[:, :nz] * factor, third[:, nz:] * factor], axis=1
                ).astype(jnp.bfloat16)
                back = jnp.dot(tx_ref[...], scaled, preferred_element_type=jnp.float32)
                freq[index, group] = back.astype(jnp.bfloat16)
            return carry

        lax.fori_loop(0, groups * HOPS, unit, 0)

    def backward(c, store):
        def unit(half, carry):
            totals = [None, None]
            for hop in range(HOPS):
                visitor = vis[hop, pl.ds(c * ROWS, ROWS)].reshape(rows, nz).astype(jnp.float32)
                spectrum = freq[
                    hop * halves + half, :, pl.ds(pl.multiple_of(c * sub, sub), sub)
                ].reshape(groups * sub, 2 * nz)
                first = jnp.dot(tyt_ref[...], spectrum, preferred_element_type=jnp.float32)
                potential = jnp.dot(
                    first.astype(jnp.bfloat16), tz_ref[...], preferred_element_type=jnp.float32
                )
                for k in range(2):
                    term = potential[:, k * nz : (k + 1) * nz] * visitor
                    totals[k] = term if hop == 0 else totals[k] + term
            for k in range(2):
                store(2 * half + k, totals[k].reshape(ROWS, ny, nz))
            return carry

        lax.fori_loop(0, halves, unit, 0)

    span = levels - 1
    ahead = 1
    for c in range(ahead):
        line_sends(c, 1, lambda copy: copy.start())
    for c in range(chunks):
        columns[c][level] = orb[mine, pl.ds(c * ROWS, ROWS)]
    for step in range(chunks + span + 1):
        if step + ahead < chunks:
            line_sends(step + ahead, 1, lambda copy: copy.start())
        for hop in range(2, span + 1):
            c = step - (hop - 1)
            if 0 <= c < chunks:
                line_arrivals(c, hop - 1)
                line_sends(c, hop, lambda copy: copy.start())
        c = step - span
        if 0 <= c < chunks:
            line_arrivals(c, span)
            send_side(c)
        c = step - span - 1
        if 0 <= c < chunks:
            side_copy(c).wait_recv()
            forward(c)

    middle()

    def core_copy(k, j):
        return pltpu.make_async_remote_copy(
            src_ref=send_core.at[k, j],
            dst_ref=recv_core.at[k, j],
            send_sem=core_send.at[k, j],
            recv_sem=core_recv.at[k, j],
            device_id=(blk, core_rep),
            device_id_type=MESH,
        )

    def chip_copy(k, j):
        return pltpu.make_async_remote_copy(
            src_ref=send_chip.at[k - 1, j],
            dst_ref=recv_chip.at[k - 1, j],
            send_sem=chip_send.at[k - 1, j],
            recv_sem=chip_recv.at[k - 1, j],
            device_id=(blk, chip_rep(k)),
            device_id_type=MESH,
        )

    for k in list(range(1, chips)) + [0]:
        home = (chip + k) % chips * CORES
        for j in range(per_slab):

            def store_core(orbital, value):
                send_core[k, j, orbital] = value.astype(jnp.bfloat16)

            backward((home + CORES - 1 - core) * per_slab + j, store_core)
            core_copy(k, j).start()
            if k > 0:

                def store_chip(orbital, value):
                    send_chip[k - 1, j, orbital] = value.astype(jnp.bfloat16)

                def store_partial(orbital, value):
                    out_ref[orbital, pl.ds(j * ROWS, ROWS)] = value

                backward((home + core) * per_slab + j, store_partial)
                core_copy(k, j).wait_recv()
                for orbital in range(n_orb):
                    store_chip(
                        orbital,
                        out_ref[orbital, pl.ds(j * ROWS, ROWS)]
                        + recv_core[k, j, orbital].astype(jnp.float32),
                    )
                chip_copy(k, j).start()
    for j in range(per_slab):

        def store_out(orbital, value):
            out_ref[orbital, pl.ds(j * ROWS, ROWS)] = value

        backward(rep * per_slab + j, store_out)
    for j in range(per_slab):
        core_copy(0, j).wait_recv()
        for k in range(1, chips):
            chip_copy(k, j).wait_recv()
        for orbital in range(n_orb):
            total = out_ref[orbital, pl.ds(j * ROWS, ROWS)]
            total = total + recv_core[0, j, orbital].astype(jnp.float32)
            for k in range(1, chips):
                total = total + recv_chip[k - 1, j, orbital].astype(jnp.float32)
            out_ref[orbital, pl.ds(j * ROWS, ROWS)] = total

    for c in range(chunks):
        for hop in range(1, span + 1):
            line_sends(c, hop, lambda copy: copy.wait_send())
        side_copy(c).wait_send()
    for j in range(per_slab):
        for k in range(chips):
            core_copy(k, j).wait_send()
        for k in range(1, chips):
            chip_copy(k, j).wait_send()


def gather_body(n_blk, n_rep, orbitals, skew):
    n_orb, nx, ny, nz = orbitals.shape
    chunks = nx // ROWS
    levels = n_blk // COLS
    chips = n_rep // CORES
    per_slab = nx // n_rep // ROWS
    groups = ny // GROUP
    bf16, f32 = jnp.bfloat16, jnp.float32

    table_z = np.kron(np.eye(2), cas_table(nz).astype(np.float32))
    table_x = np.kron(cas_table(nx).astype(np.float32), np.eye(GROUP))
    table_y = np.einsum(
        "gky,xw->gxkwy",
        cas_table(ny).astype(np.float32).reshape(groups, GROUP, ny),
        np.eye(ROWS, dtype=np.float32),
    ).reshape(ROWS * ny, ROWS * ny)
    kernel = (
        kernel_table(nx, ny, nz)
        .reshape(nx, groups, GROUP, nz)
        .transpose(1, 0, 2, 3)
        .reshape(groups, nx * GROUP, nz)
    )
    others = HOPS // COLS
    dma = pltpu.SemaphoreType.DMA
    piece = (ROWS, ny, nz)
    scratch = (
        [pltpu.VMEM((levels, *piece), bf16) for _ in range(chunks)]
        + [pltpu.VMEM((others, *piece), bf16) for _ in range(2 * chunks)]
        + [
            pltpu.VMEM((HOPS, nx, ny, nz), bf16),
            pltpu.VMEM((HOPS * n_orb // 2, groups, nx * GROUP, 2 * nz), bf16),
            pltpu.VMEM((chips, per_slab, n_orb, *piece), bf16),
            pltpu.VMEM((chips, per_slab, n_orb, *piece), bf16),
            pltpu.VMEM((max(chips - 1, 1), per_slab, n_orb, *piece), bf16),
            pltpu.VMEM((max(chips - 1, 1), per_slab, n_orb, *piece), bf16),
            dma((chunks, max(levels - 1, 1), 2)),
            dma((chunks, max(levels - 1, 1), 2)),
            dma((chunks,)),
            dma((chunks,)),
            dma((chips, per_slab)),
            dma((chips, per_slab)),
            dma((max(chips - 1, 1), per_slab)),
            dma((max(chips - 1, 1), per_slab)),
        ]
    )
    vmem = pl.BlockSpec(memory_space=pltpu.VMEM)
    pairs = HOPS * n_orb
    return pl.pallas_call(
        functools.partial(fields_kernel, n_blk, n_rep),
        out_shape=jax.ShapeDtypeStruct((n_orb, nx // n_rep, ny, nz), f32),
        in_specs=[pl.BlockSpec(memory_space=pltpu.SMEM)] + [vmem] * 6,
        out_specs=vmem,
        scratch_shapes=scratch,
        compiler_params=pltpu.CompilerParams(
            collective_id=0, has_side_effects=True, vmem_limit_bytes=48 * 1024 * 1024
        ),
        cost_estimate=pl.CostEstimate(
            flops=4 * pairs * nx * ny * nz * (nx + ny + nz),
            bytes_accessed=2 * n_orb * nx * ny * nz,
            transcendentals=0,
        ),
    )(
        skew,
        orbitals,
        jnp.asarray(table_z, bf16),
        jnp.asarray(table_y, bf16),
        jnp.asarray(table_y.T, bf16),
        jnp.asarray(table_x, bf16),
        jnp.asarray(kernel),
    )


def solution(mesh):
    n_blk, n_rep = mesh.shape["blk"], mesh.shape["rep"]
    few = n_blk <= HOPS * COLS and n_blk % COLS == 0 and n_rep % CORES == 0
    body = functools.partial(gather_body, n_blk, n_rep) if few else shift_body
    placed = (P("blk", None, None, None), P("rep"))
    return jax.shard_map(
        body, mesh=mesh, in_specs=placed, out_specs=P("blk", "rep", None, None), check_vma=False
    )
```

time: 190 us -> 77 us (0.41)
  waiting for transfers between devices: 89.6 us -> 0 us
  Pallas kernels: 0 us -> 69.1 us
  matrix products: 56.5 us -> 0 us
  other arithmetic: 16.1 us -> 0 us
  between operations: 14.2 us -> 0.67 us
  starting transfers between devices: 3.13 us -> 0 us
  local copies, waits for them, and re-layouts: 9.37 us -> 7.01 us
    pallas_call x0 -> x1, Pallas kernels: none -> 69.1 us  [gather_body(): pl.pallas_call(functools.partial(fields_kernel, n_blk, n_rep), out_shape=...]
    dot_general x16 -> x0, matrix products: 56.5 us -> none  [the longest x8 28.3 us: transform(): jnp.einsum('oxyz,yk->oxkz', first, table_y, preferred_element_type=jnp.fl...]
    ppermute x6 -> x0, waiting for transfers between devices: 51.7 us -> none  [shifted_2(): return lax.ppermute(value, axis, pairs)]
    reduce_scatter x1 -> x0, waiting for transfers between devices: 37.8 us -> none  [body(): return lax.psum_scatter(field_sum, 'rep', scatter_dimension=1, tiled=True)]
    convert_element_type x5 -> x0, other arithmetic: 13.6 us -> none  [the longest x1 8.97 us: pair_field(): scaled = (kernel[None] * forward.astype(jnp.float32)).astype(jnp.bfloat16)]
    unnamed x8 -> x13, local copies, waits for them, and re-layouts: 1.17 us -> 7.01 us
    convert_element_type x4 -> x0, local copies, waits for them, and re-layouts: 5.03 us -> none  [pair_field(): visitor.astype(jnp.float32)[None]]
    ppermute x6 -> x0, starting transfers between devices: 3.13 us -> none  [shifted_2(): return lax.ppermute(value, axis, pairs)]
  transfers between devices with their start and end apart: 7 -> 0, of which waited for: 7 -> 0; matrix products, arithmetic and copies ran while one was open for 15% -> 0% of each run, Pallas kernels for 0% -> 0%
where the time goes in v1:
time: 77 us; the launch traced here: 76.7 us
  Pallas kernels  69.1 us (90%)
  local copies, waits for them, and re-layouts  7.01 us (9%)
    pallas_call x1, Pallas kernels, gather_body(): pl.pallas_call(functools.partial(fields_kernel, n_blk, n_rep), out_shape=...  69.1 us
    unnamed x13, local copies, waits for them, and re-layouts  7.01 us

profile of v1, /device:TPU:0, one launch (start us, length us, event | category | flops | bytes accessed | tf_op | source)
XLA Modules:
  0.0 76.7 jit_solution(6683243554578640709)
XLA Ops:
  0.7 0.0 copy-start
  0.7 1.4 %copy-done = bf16[4,32,48,128]{3,2,1,0:T(8,128)(2,1)S(1)} copy-done((bf16[4,32,48,128]{3,2,1,0:T(8,128)(2,1)S(1)}, bf16[4,32,48,128]{3,2,1,0:T(8,128)(2,1)}, u32[]{:S(2)}) %copy-start) | copy-done | bytes 1572888
  2.1 0.0 copy-start.1
  2.1 1.1 %copy-done.1 = f32[6,256,128]{2,1,0:T(8,128)S(1)} copy-done((f32[6,256,128]{2,1,0:T(8,128)S(1)}, f32[6,256,128]{2,1,0:T(8,128)}, u32[]{:S(2)}) %copy-start.1) | copy-done | bytes 786456
  3.2 0.0 copy-start.2
  3.2 0.9 %copy-done.2 = bf16[256,256]{1,0:T(8,128)(2,1)S(1)} copy-done((bf16[256,256]{1,0:T(8,128)(2,1)S(1)}, bf16[256,256]{1,0:T(8,128)(2,1)}, u32[]{:S(2)}) %copy-start.2) | copy-done | bytes 131096
  4.1 0.0 copy-start.3
  4.1 0.9 %copy-done.3 = bf16[256,256]{1,0:T(8,128)(2,1)S(1)} copy-done((bf16[256,256]{1,0:T(8,128)(2,1)S(1)}, bf16[256,256]{1,0:T(8,128)(2,1)}, u32[]{:S(2)}) %copy-start.3) | copy-done | bytes 131096
  5.0 0.0 copy-start.4
  5.0 0.9 %copy-done.4 = bf16[192,192]{1,0:T(8,128)(2,1)S(1)} copy-done((bf16[192,192]{1,0:T(8,128)(2,1)S(1)}, bf16[192,192]{1,0:T(8,128)(2,1)}, u32[]{:S(2)}) %copy-start.4) | copy-done | bytes 73752
  5.9 0.0 copy-start.5
  5.9 0.9 %copy-done.5 = bf16[192,192]{1,0:T(8,128)(2,1)S(1)} copy-done((bf16[192,192]{1,0:T(8,128)(2,1)S(1)}, bf16[192,192]{1,0:T(8,128)(2,1)}, u32[]{:S(2)}) %copy-start.5) | copy-done | bytes 73752
  6.8 69.1 %shard_map.73 = f32[4,8,48,128]{3,2,1,0:T(8,128)S(1)} custom-call(s32[1]{0:T(128)S(6)} %copy.9.skew_ref, bf16[4,32,48,128]{3,2,1,0:T(8,128)(2,1)S(1)} %copy-done, bf16[256,256]{1,0:T(8,128)(2,1)S(1)} %copy-done.3, bf16[192,192]{1,0:T(8,128)(2,1)S(1)} %copy-done.5, bf16[192,192]{1,0:T(8,128)(2,1)S(1)} %copy-done.4, bf16[256,256]{1,0:T(8,128)(2,1)S(1)} %copy-done.2, ...), custom_call_target="tpu_custom_call" | custom-call | flops 2617245696 | bytes 1572864 | tf_op jit(solution)/shard_map/pallas_call | solution.py:423
  75.9 0.9 %copy.10 = f32[4,8,48,128]{3,2,1,0:T(8,128)} copy(f32[4,8,48,128]{3,2,1,0:T(8,128)S(1)} %shard_map.73) | data formatting | bytes 1572864
Async XLA Ops:
  0.7 1.4 %copy-start = (bf16[4,32,48,128]{3,2,1,0:T(8,128)(2,1)S(1)}, bf16[4,32,48,128]{3,2,1,0:T(8,128)(2,1)}, u32[]{:S(2)}) copy-start(bf16[4,32,48,128]{3,2,1,0:T(8,128)(2,1)} %orb.1) | copy-start | bytes 4718596
  2.1 1.1 %copy-start.1 = (f32[6,256,128]{2,1,0:T(8,128)S(1)}, f32[6,256,128]{2,1,0:T(8,128)}, u32[]{:S(2)}) copy-start(f32[6,256,128]{2,1,0:T(8,128)} %constant.14.clone.kern_ref) | copy-start | bytes 2359300
  3.2 0.9 %copy-start.2 = (bf16[256,256]{1,0:T(8,128)(2,1)S(1)}, bf16[256,256]{1,0:T(8,128)(2,1)}, u32[]{:S(2)}) copy-start(bf16[256,256]{1,0:T(8,128)(2,1)} %constant.13.clone.tx_ref) | copy-start | bytes 393220
  4.1 0.9 %copy-start.3 = (bf16[256,256]{1,0:T(8,128)(2,1)S(1)}, bf16[256,256]{1,0:T(8,128)(2,1)}, u32[]{:S(2)}) copy-start(bf16[256,256]{1,0:T(8,128)(2,1)} %constant.10.clone.tz_ref) | copy-start | bytes 393220
  5.0 0.9 %copy-start.4 = (bf16[192,192]{1,0:T(8,128)(2,1)S(1)}, bf16[192,192]{1,0:T(8,128)(2,1)}, u32[]{:S(2)}) copy-start(bf16[192,192]{1,0:T(8,128)(2,1)} %constant.12.clone.tyt_ref) | copy-start | bytes 221188
  5.9 0.9 %copy-start.5 = (bf16[192,192]{1,0:T(8,128)(2,1)S(1)}, bf16[192,192]{1,0:T(8,128)(2,1)}, u32[]{:S(2)}) copy-start(bf16[192,192]{1,0:T(8,128)(2,1)} %constant.11.clone.ty_ref) | copy-start | bytes 221188

commit v2 on v1

--- a/solution.py
+++ b/solution.py
@@ -96,9 +96,9 @@
 
 
 def fields_kernel(
-    n_blk, n_rep, skew_ref, orb, tz_ref, ty_ref, tyt_ref, tx_ref, kern_ref, out_ref, *scratch
+    n_blk, n_rep, skew_ref, orb_hbm, tz_hbm, ty_hbm, tyt_hbm, tx_hbm, kern_hbm, out_ref, *scratch
 ):
-    n_orb, nx, ny, nz = orb.shape
+    n_orb, nx, ny, nz = orb_hbm.shape
     chunks = nx // ROWS
     levels = n_blk // COLS
     chips = n_rep // CORES
@@ -112,6 +112,8 @@
     staged = scratch[chunks : 2 * chunks]
     sides = scratch[2 * chunks : 3 * chunks]
     scratch = scratch[3 * chunks :]
+    orb, tz_ref, ty_ref, tyt_ref, tx_ref, kern_ref, load_sem = scratch[:7]
+    scratch = scratch[7:]
     vis, freq, send_core, recv_core, send_chip, recv_chip = scratch[:6]
     line_send, line_recv, side_send, side_recv, core_send, core_recv, chip_send, chip_recv = scratch[
         6:
@@ -129,6 +131,21 @@
     def chip_rep(step):
         return (chip + step) % chips * CORES + core
 
+    loads = [
+        pltpu.make_async_copy(src, dst, load_sem.at[i])
+        for i, (src, dst) in enumerate(
+            [
+                (orb_hbm, orb),
+                (tz_hbm, tz_ref),
+                (ty_hbm, ty_ref),
+                (tx_hbm, tx_ref),
+                (kern_hbm, kern_ref),
+                (tyt_hbm, tyt_ref),
+            ]
+        )
+    ]
+    for load in loads:
+        load.start()
     barrier = pltpu.get_barrier_semaphore()
     pl.semaphore_signal(barrier, inc=1, device_id=(side_blk, rep), device_id_type=MESH)
     pl.semaphore_signal(barrier, inc=1, device_id=(blk, core_rep), device_id_type=MESH)
@@ -150,7 +167,7 @@
         source = level - (hop - 1) if up else level + (hop - 1)
         way = 0 if up else 1
         if hop == 1:
-            src = orb.at[mine, pl.ds(c * ROWS, ROWS)]
+            src = orb_hbm.at[mine, pl.ds(c * ROWS, ROWS)]
         else:
             src = columns[c].at[source]
         return pltpu.make_async_remote_copy(
@@ -214,7 +231,7 @@
                 owner % COLS == col, columns[c][owner // COLS], sides[c][hop // COLS]
             )
 
-        def unit(hop, carry):
+        for hop in range(HOPS):
             visitor = vis[hop, pl.ds(c * ROWS, ROWS)].reshape(rows, nz)
             for half in range(halves):
                 density = jnp.concatenate(
@@ -231,15 +248,11 @@
                 freq[hop * halves + half, :, pl.ds(c * sub, sub)] = second.astype(
                     jnp.bfloat16
                 ).reshape(groups, sub, 2 * nz)
-            return carry
-
-        lax.fori_loop(0, HOPS, unit, 0)
-
-    def middle():
-        def unit(step, carry):
-            group, hop = step // HOPS, step % HOPS
+
+    def middle(half):
+        def unit(group, carry):
             factor = kern_ref[group]
-            for half in range(halves):
+            for hop in range(HOPS):
                 index = hop * halves + half
                 third = jnp.dot(
                     tx_ref[...], freq[index, group], preferred_element_type=jnp.float32
@@ -251,33 +264,31 @@
                 freq[index, group] = back.astype(jnp.bfloat16)
             return carry
 
-        lax.fori_loop(0, groups * HOPS, unit, 0)
-
-    def backward(c, store):
-        def unit(half, carry):
-            totals = [None, None]
-            for hop in range(HOPS):
-                visitor = vis[hop, pl.ds(c * ROWS, ROWS)].reshape(rows, nz).astype(jnp.float32)
-                spectrum = freq[
-                    hop * halves + half, :, pl.ds(pl.multiple_of(c * sub, sub), sub)
-                ].reshape(groups * sub, 2 * nz)
-                first = jnp.dot(tyt_ref[...], spectrum, preferred_element_type=jnp.float32)
-                potential = jnp.dot(
-                    first.astype(jnp.bfloat16), tz_ref[...], preferred_element_type=jnp.float32
-                )
-                for k in range(2):
-                    term = potential[:, k * nz : (k + 1) * nz] * visitor
-                    totals[k] = term if hop == 0 else totals[k] + term
+        lax.fori_loop(0, groups, unit, 0)
+
+    def backward(c, half, store):
+        totals = [None, None]
+        for hop in range(HOPS):
+            visitor = vis[hop, pl.ds(c * ROWS, ROWS)].reshape(rows, nz).astype(jnp.float32)
+            spectrum = freq[
+                hop * halves + half, :, pl.ds(pl.multiple_of(c * sub, sub), sub)
+            ].reshape(groups * sub, 2 * nz)
+            first = jnp.dot(tyt_ref[...], spectrum, preferred_element_type=jnp.float32)
+            potential = jnp.dot(
+                first.astype(jnp.bfloat16), tz_ref[...], preferred_element_type=jnp.float32
+            )
             for k in range(2):
-                store(2 * half + k, totals[k].reshape(ROWS, ny, nz))
-            return carry
-
-        lax.fori_loop(0, halves, unit, 0)
+                term = potential[:, k * nz : (k + 1) * nz] * visitor
+                totals[k] = term if hop == 0 else totals[k] + term
+        for k in range(2):
+            store(2 * half + k, totals[k].reshape(ROWS, ny, nz))
 
     span = levels - 1
-    ahead = 1
+    ahead = 2
     for c in range(ahead):
         line_sends(c, 1, lambda copy: copy.start())
+    for load in loads:
+        load.wait()
     for c in range(chunks):
         columns[c][level] = orb[mine, pl.ds(c * ROWS, ROWS)]
     for step in range(chunks + span + 1):
@@ -297,80 +308,83 @@
             side_copy(c).wait_recv()
             forward(c)
 
-    middle()
-
-    def core_copy(k, j):
+    def core_copy(k, j, half):
+        both = pl.ds(2 * half, 2)
         return pltpu.make_async_remote_copy(
-            src_ref=send_core.at[k, j],
-            dst_ref=recv_core.at[k, j],
-            send_sem=core_send.at[k, j],
-            recv_sem=core_recv.at[k, j],
+            src_ref=send_core.at[k, j, both],
+            dst_ref=recv_core.at[k, j, both],
+            send_sem=core_send.at[k, j, half],
+            recv_sem=core_recv.at[k, j, half],
             device_id=(blk, core_rep),
             device_id_type=MESH,
         )
 
-    def chip_copy(k, j):
+    def chip_copy(k, j, half):
+        both = pl.ds(2 * half, 2)
         return pltpu.make_async_remote_copy(
-            src_ref=send_chip.at[k - 1, j],
-            dst_ref=recv_chip.at[k - 1, j],
-            send_sem=chip_send.at[k - 1, j],
-            recv_sem=chip_recv.at[k - 1, j],
+            src_ref=send_chip.at[k - 1, j, both],
+            dst_ref=recv_chip.at[k - 1, j, both],
+            send_sem=chip_send.at[k - 1, j, half],
+            recv_sem=chip_recv.at[k - 1, j, half],
             device_id=(blk, chip_rep(k)),
             device_id_type=MESH,
         )
 
-    for k in list(range(1, chips)) + [0]:
-        home = (chip + k) % chips * CORES
+    def finish(half):
         for j in range(per_slab):
-
-            def store_core(orbital, value):
-                send_core[k, j, orbital] = value.astype(jnp.bfloat16)
-
-            backward((home + CORES - 1 - core) * per_slab + j, store_core)
-            core_copy(k, j).start()
-            if k > 0:
-
-                def store_chip(orbital, value):
-                    send_chip[k - 1, j, orbital] = value.astype(jnp.bfloat16)
+            core_copy(0, j, half).wait_recv()
+            for k in range(1, chips):
+                chip_copy(k, j, half).wait_recv()
+            for orbital in range(2 * half, 2 * half + 2):
+                total = out_ref[orbital, pl.ds(j * ROWS, ROWS)]
+                total = total + recv_core[0, j, orbital].astype(jnp.float32)
+                for k in range(1, chips):
+                    total = total + recv_chip[k - 1, j, orbital].astype(jnp.float32)
+                out_ref[orbital, pl.ds(j * ROWS, ROWS)] = total
+
+    for half in range(halves):
+        middle(half)
+        for k in list(range(1, chips)) + [0]:
+            home = (chip + k) % chips * CORES
+            for j in range(per_slab):
+
+                def store_core(orbital, value):
+                    send_core[k, j, orbital] = value.astype(jnp.bfloat16)
+
+                backward((home + CORES - 1 - core) * per_slab + j, half, store_core)
+                core_copy(k, j, half).start()
+            for j in range(per_slab if k > 0 else 0):
 
                 def store_partial(orbital, value):
                     out_ref[orbital, pl.ds(j * ROWS, ROWS)] = value
 
-                backward((home + core) * per_slab + j, store_partial)
-                core_copy(k, j).wait_recv()
-                for orbital in range(n_orb):
-                    store_chip(
-                        orbital,
+                backward((home + core) * per_slab + j, half, store_partial)
+                core_copy(k, j, half).wait_recv()
+                for orbital in range(2 * half, 2 * half + 2):
+                    send_chip[k - 1, j, orbital] = (
                         out_ref[orbital, pl.ds(j * ROWS, ROWS)]
-                        + recv_core[k, j, orbital].astype(jnp.float32),
-                    )
-                chip_copy(k, j).start()
-    for j in range(per_slab):
-
-        def store_out(orbital, value):
-            out_ref[orbital, pl.ds(j * ROWS, ROWS)] = value
-
-        backward(rep * per_slab + j, store_out)
-    for j in range(per_slab):
-        core_copy(0, j).wait_recv()
-        for k in range(1, chips):
-            chip_copy(k, j).wait_recv()
-        for orbital in range(n_orb):
-            total = out_ref[orbital, pl.ds(j * ROWS, ROWS)]
-            total = total + recv_core[0, j, orbital].astype(jnp.float32)
-            for k in range(1, chips):
-                total = total + recv_chip[k - 1, j, orbital].astype(jnp.float32)
-            out_ref[orbital, pl.ds(j * ROWS, ROWS)] = total
+                        + recv_core[k, j, orbital].astype(jnp.float32)
+                    ).astype(jnp.bfloat16)
+                chip_copy(k, j, half).start()
+        for j in range(per_slab):
+
+            def store_out(orbital, value):
+                out_ref[orbital, pl.ds(j * ROWS, ROWS)] = value
+
+            backward(rep * per_slab + j, half, store_out)
+    for half in range(halves):
+        finish(half)
 
     for c in range(chunks):
         for hop in range(1, span + 1):
             line_sends(c, hop, lambda copy: copy.wait_send())
         side_copy(c).wait_send()
-    for j in range(per_slab):
-        for k in range(chips):
-            core_copy(k, j).wait_send()
-        for k in range(1, chips):
-            chip_copy(k, j).wait_send()
+    for half in range(halves):
+        for j in range(per_slab):
+            for k in range(chips):
+                core_copy(k, j, half).wait_send()
+            for k in range(1, chips):
+                chip_copy(k, j, half).wait_send()
 
 
 def gather_body(n_blk, n_rep, orbitals, skew):
@@ -402,6 +416,13 @@
         [pltpu.VMEM((levels, *piece), bf16) for _ in range(chunks)]
         + [pltpu.VMEM((others, *piece), bf16) for _ in range(2 * chunks)]
         + [
+            pltpu.VMEM((n_orb, nx, ny, nz), bf16),
+            pltpu.VMEM(table_z.shape, bf16),
+            pltpu.VMEM(table_y.shape, bf16),
+            pltpu.VMEM(table_y.shape, bf16),
+            pltpu.VMEM(table_x.shape, bf16),
+            pltpu.VMEM(kernel.shape, f32),
+            dma((6,)),
             pltpu.VMEM((HOPS, nx, ny, nz), bf16),
             pltpu.VMEM((HOPS * n_orb // 2, groups, nx * GROUP, 2 * nz), bf16),
             pltpu.VMEM((chips, per_slab, n_orb, *piece), bf16),
@@ -412,10 +433,10 @@
             dma((chunks, max(levels - 1, 1), 2)),
             dma((chunks,)),
             dma((chunks,)),
-            dma((chips, per_slab)),
-            dma((chips, per_slab)),
-            dma((max(chips - 1, 1), per_slab)),
-            dma((max(chips - 1, 1), per_slab)),
+            dma((chips, per_slab, n_orb // 2)),
+            dma((chips, per_slab, n_orb // 2)),
+            dma((max(chips - 1, 1), per_slab, n_orb // 2)),
+            dma((max(chips - 1, 1), per_slab, n_orb // 2)),
         ]
     )
     vmem = pl.BlockSpec(memory_space=pltpu.VMEM)
@@ -423,7 +444,8 @@
     return pl.pallas_call(
         functools.partial(fields_kernel, n_blk, n_rep),
         out_shape=jax.ShapeDtypeStruct((n_orb, nx // n_rep, ny, nz), f32),
-        in_specs=[pl.BlockSpec(memory_space=pltpu.SMEM)] + [vmem] * 6,
+        in_specs=[pl.BlockSpec(memory_space=pltpu.SMEM)]
+        + [pl.BlockSpec(memory_space=pltpu.HBM)] * 6,
         out_specs=vmem,
         scratch_shapes=scratch,
         compiler_params=pltpu.CompilerParams(

time: 77 us -> 68.8 us (0.89)
  Pallas kernels: 69.1 us -> 60.9 us
    pallas_call x1, Pallas kernels: 69.1 us -> 60.9 us  [gather_body(): pl.pallas_call(functools.partial(fields_kernel, n_blk, n_rep), out_shape=...]
where the time goes in v2:
time: 68.8 us; the launch traced here: 68.6 us
  Pallas kernels  60.9 us (89%)
  local copies, waits for them, and re-layouts  7.01 us (10%)
    pallas_call x1, Pallas kernels, gather_body(): pl.pallas_call(functools.partial(fields_kernel, n_blk, n_rep), out_shape=...  60.9 us
    unnamed x13, local copies, waits for them, and re-layouts  7.01 us

profile of v2, /device:TPU:0, one launch (start us, length us, event | category | flops | bytes accessed | tf_op | source)
XLA Modules:
  0.0 68.6 jit_solution(4131962720586570971)
XLA Ops:
  0.7 0.0 copy-start
  0.7 1.4 %copy-done = bf16[4,32,48,128]{3,2,1,0:T(8,128)(2,1)S(1)} copy-done((bf16[4,32,48,128]{3,2,1,0:T(8,128)(2,1)S(1)}, bf16[4,32,48,128]{3,2,1,0:T(8,128)(2,1)}, u32[]{:S(2)}) %copy-start) | copy-done | bytes 1572888
  2.1 0.0 copy-start.1
  2.1 1.1 %copy-done.1 = f32[6,256,128]{2,1,0:T(8,128)S(1)} copy-done((f32[6,256,128]{2,1,0:T(8,128)S(1)}, f32[6,256,128]{2,1,0:T(8,128)}, u32[]{:S(2)}) %copy-start.1) | copy-done | bytes 786456
  3.2 0.0 copy-start.2
  3.2 0.9 %copy-done.2 = bf16[256,256]{1,0:T(8,128)(2,1)S(1)} copy-done((bf16[256,256]{1,0:T(8,128)(2,1)S(1)}, bf16[256,256]{1,0:T(8,128)(2,1)}, u32[]{:S(2)}) %copy-start.2) | copy-done | bytes 131096
  4.1 0.0 copy-start.3
  4.1 0.9 %copy-done.3 = bf16[256,256]{1,0:T(8,128)(2,1)S(1)} copy-done((bf16[256,256]{1,0:T(8,128)(2,1)S(1)}, bf16[256,256]{1,0:T(8,128)(2,1)}, u32[]{:S(2)}) %copy-start.3) | copy-done | bytes 131096
  5.0 0.0 copy-start.4
  5.0 0.9 %copy-done.4 = bf16[192,192]{1,0:T(8,128)(2,1)S(1)} copy-done((bf16[192,192]{1,0:T(8,128)(2,1)S(1)}, bf16[192,192]{1,0:T(8,128)(2,1)}, u32[]{:S(2)}) %copy-start.4) | copy-done | bytes 73752
  5.9 0.0 copy-start.5
  5.9 0.9 %copy-done.5 = bf16[192,192]{1,0:T(8,128)(2,1)S(1)} copy-done((bf16[192,192]{1,0:T(8,128)(2,1)S(1)}, bf16[192,192]{1,0:T(8,128)(2,1)}, u32[]{:S(2)}) %copy-start.5) | copy-done | bytes 73752
  6.8 60.9 %shard_map.73 = f32[4,8,48,128]{3,2,1,0:T(8,128)S(1)} custom-call(s32[1]{0:T(128)S(6)} %copy.9.skew_ref, bf16[4,32,48,128]{3,2,1,0:T(8,128)(2,1)S(1)} %copy-done, bf16[256,256]{1,0:T(8,128)(2,1)S(1)} %copy-done.3, bf16[192,192]{1,0:T(8,128)(2,1)S(1)} %copy-done.5, bf16[192,192]{1,0:T(8,128)(2,1)S(1)} %copy-done.4, bf16[256,256]{1,0:T(8,128)(2,1)S(1)} %copy-done.2, ...), custom_call_target="tpu_custom_call" | custom-call | flops 2617245696 | bytes 1572864 | tf_op jit(solution)/shard_map/pallas_call | solution.py:444
  67.7 0.9 %copy.10 = f32[4,8,48,128]{3,2,1,0:T(8,128)} copy(f32[4,8,48,128]{3,2,1,0:T(8,128)S(1)} %shard_map.73) | data formatting | bytes 1572864
Async XLA Ops:
  0.7 1.4 %copy-start = (bf16[4,32,48,128]{3,2,1,0:T(8,128)(2,1)S(1)}, bf16[4,32,48,128]{3,2,1,0:T(8,128)(2,1)}, u32[]{:S(2)}) copy-start(bf16[4,32,48,128]{3,2,1,0:T(8,128)(2,1)} %orb_hbm.1) | copy-start | bytes 4718596
  2.1 1.1 %copy-start.1 = (f32[6,256,128]{2,1,0:T(8,128)S(1)}, f32[6,256,128]{2,1,0:T(8,128)}, u32[]{:S(2)}) copy-start(f32[6,256,128]{2,1,0:T(8,128)} %constant.14.clone.kern_hbm) | copy-start | bytes 2359300
  3.2 0.9 %copy-start.2 = (bf16[256,256]{1,0:T(8,128)(2,1)S(1)}, bf16[256,256]{1,0:T(8,128)(2,1)}, u32[]{:S(2)}) copy-start(bf16[256,256]{1,0:T(8,128)(2,1)} %constant.13.clone.tx_hbm) | copy-start | bytes 393220
  4.1 0.9 %copy-start.3 = (bf16[256,256]{1,0:T(8,128)(2,1)S(1)}, bf16[256,256]{1,0:T(8,128)(2,1)}, u32[]{:S(2)}) copy-start(bf16[256,256]{1,0:T(8,128)(2,1)} %constant.10.clone.tz_hbm) | copy-start | bytes 393220
  5.0 0.9 %copy-start.4 = (bf16[192,192]{1,0:T(8,128)(2,1)S(1)}, bf16[192,192]{1,0:T(8,128)(2,1)}, u32[]{:S(2)}) copy-start(bf16[192,192]{1,0:T(8,128)(2,1)} %constant.12.clone.tyt_hbm) | copy-start | bytes 221188
  5.9 0.9 %copy-start.5 = (bf16[192,192]{1,0:T(8,128)(2,1)S(1)}, bf16[192,192]{1,0:T(8,128)(2,1)}, u32[]{:S(2)}) copy-start(bf16[192,192]{1,0:T(8,128)(2,1)} %constant.11.clone.ty_hbm) | copy-start | bytes 221188

commit v3 on v2

--- a/solution.py
+++ b/solution.py
@@ -449,7 +449,7 @@
         out_specs=vmem,
         scratch_shapes=scratch,
         compiler_params=pltpu.CompilerParams(
-            collective_id=0, has_side_effects=True, vmem_limit_bytes=48 * 1024 * 1024
+            collective_id=0, has_side_effects=True, vmem_limit_bytes=64 * 1024 * 1024 - 64 * 1024
         ),
         cost_estimate=pl.CostEstimate(
             flops=4 * pairs * nx * ny * nz * (nx + ny + nz),

time: 68.8 us -> 64.5 us (0.938)
  local copies, waits for them, and re-layouts: 7.01 us -> 2.09 us
  Pallas kernels: 60.9 us -> 61.6 us
    unnamed x13 -> x1, local copies, waits for them, and re-layouts: 7.01 us -> 2.09 us
    pallas_call x1, Pallas kernels: 60.9 us -> 61.6 us  [gather_body(): pl.pallas_call(functools.partial(fields_kernel, n_blk, n_rep), out_shape=...]
where the time goes in v3:
time: 64.5 us; the launch traced here: 64.3 us
  Pallas kernels  61.6 us (96%)
  local copies, waits for them, and re-layouts  2.09 us (3%)
  between operations  0.66 us (1%)
    pallas_call x1, Pallas kernels, gather_body(): pl.pallas_call(functools.partial(fields_kernel, n_blk, n_rep), out_shape=...  61.6 us
    unnamed x1, local copies, waits for them, and re-layouts  2.09 us

profile of v3, /device:TPU:0, one launch (start us, length us, event | category | flops | bytes accessed | tf_op | source)
XLA Modules:
  0.0 64.3 jit_solution(10056397919536204496)
XLA Ops:
  0.7 61.6 %shard_map.73 = f32[4,8,48,128]{3,2,1,0:T(8,128)} custom-call(s32[1]{0:T(128)S(6)} %copy.9.skew_ref, bf16[4,32,48,128]{3,2,1,0:T(8,128)(2,1)} %orb_hbm.1, bf16[256,256]{1,0:T(8,128)(2,1)} %constant.10.clone.tz_hbm, bf16[192,192]{1,0:T(8,128)(2,1)} %constant.11.clone.ty_hbm, bf16[192,192]{1,0:T(8,128)(2,1)} %constant.12.clone.tyt_hbm, ...), custom_call_target="tpu_custom_call" | custom-call | flops 2617245696 | bytes 1572864 | tf_op jit(solution)/shard_map/pallas_call | solution.py:444
  62.2 2.1 %copy.10 = f32[4,8,48,128]{3,2,1,0:T(8,128)} copy(f32[4,8,48,128]{3,2,1,0:T(8,128)} %shard_map.73) | data formatting | bytes 1572864
